TPU v7x, 512 devices: a whole 4x4x16 slice. The times are simulated.
512 devices in a mesh: af: 4 (over x), ga: 8 (over y, core), ha: 16 (over z).
Axes of the slice: x: 4, y: 4, z: 16, core: 2. Of those that a mesh axis runs over, the one named last changes fastest.
Arguments:
- field: float32 [512, 256, 2048], P('af', 'ga', 'ha'), may hold values from -33 to 33, as said below
- start: float32 [512, 64], replicated, may hold values from -6 to 6
Outputs:
- core: float32 [64, 256, 2048], P('af', 'ga', 'ha')
Inputs may be any that keep to these rules, and one draw needn't show every extreme that they name: `field`: real values.
All inputs are finite; a program needn't handle non-finite values.
Results may differ from a plain program's by a relative error of at most 0.0003.
Values sent between devices are 32-bit elements; how exact they have to be, the bound alone decides.
A program may use at most 64 MiB of HBM per device.

v0:
```python
import jax
import jax.numpy as jnp
from jax import lax
from jax.sharding import PartitionSpec as P

ITERS = 6


def orthonormal(work):
    highest = lax.Precision.HIGHEST
    inner = jnp.dot(work.T, work, precision=highest, preferred_element_type=jnp.float32)
    lower = jnp.linalg.cholesky(inner)
    return lax.linalg.triangular_solve(lower, work, left_side=False, lower=True, transpose_a=True)


def per_device(field, start):
    highest = lax.Precision.HIGHEST
    rows_local, second, cells = field.shape
    groups = lax.axis_size("af")
    total_rows = rows_local * groups
    ncols = second * cells * lax.axis_size("ga") * lax.axis_size("ha")
    fibres = lax.all_to_all(field, "af", split_axis=1, concat_axis=0, tiled=True)
    columns = fibres.reshape(total_rows, -1)
    partial_gram = jnp.dot(
        columns, columns.T, precision=highest, preferred_element_type=jnp.float32
    )
    basis = start
    gram = lax.psum(partial_gram, ("af", "ga", "ha")) * (1.0 / ncols)
    for step in range(ITERS):
        work = jnp.dot(gram, basis, precision=highest, preferred_element_type=jnp.float32)
        basis = orthonormal(work)
    projected = jnp.dot(basis.T, columns, precision=highest, preferred_element_type=jnp.float32)
    projected = projected.reshape(basis.shape[1], second // groups, cells)
    return lax.all_to_all(projected, "af", split_axis=0, concat_axis=1, tiled=True)


def solution(mesh):
    placed = (P("af", "ga", "ha"), P())
    return jax.shard_map(
        per_device, mesh=mesh, in_specs=placed, out_specs=P("af", "ga", "ha"), check_vma=False
    )
```

profile of v0, /device:TPU:1, one launch (start us, length us, event | category | flops | bytes accessed | tf_op | source)
XLA Modules:
  0.0 621.5 jit_solution(13062133446050169936)
XLA Ops:
  6.5 2.8 copy.11
  9.4 25.8 %all_to_all.33 = f32[128,32,128]{2,0,1:T(8,128)} all-to-all(f32[128,32,128]{2,0,1:T(8,128)S(1)} %copy.11), channel_id=1, replica_groups=mesh['af'=4,'ga'=8,'ha'=16] {'af'}, dimensions={1} | all-to-all | bytes 4194304 | tf_op jit(solution)/shard_map/all_to_all | solution.py:22
  35.1 2.0 copy.12
  37.2 4.5 fusion.52
  41.8 1.8 copy.25
  43.5 473.6 %all-reduce.2.cloned.1.call-done = f32[512,512]{1,0:T(8,128)} async-done(((f32[512,512]{1,0:T(8,128)}), f32[512,512]{1,0:T(8,128)}) %all-reduce.2.cloned.1.call-update) | async-done | bytes 1048592 | tf_op jit(solution)/shard_map/psum | solution.py:28
  517.1 2.5 fusion.10
  519.9 5.8 cholesky.104
  526.5 0.7 fusion.18
  527.1 4.9 custom-call.10
  532.4 1.2 fusion.8
  533.9 5.8 cholesky.115
  540.4 0.7 fusion.19
  541.1 4.9 custom-call.11
  546.3 1.2 fusion.6
  547.9 6.0 cholesky.126
  555.2 4.9 custom-call.12
  560.4 1.2 fusion.4
  561.9 5.8 cholesky.137
  568.4 0.7 fusion.21
  569.1 4.9 custom-call.13
  574.3 1.2 fusion.2
  575.9 5.8 cholesky.148
  582.4 0.7 fusion.22
  583.1 4.9 custom-call.14
  588.3 1.2 fusion
  589.8 5.8 cholesky.159
  596.4 0.7 fusion.23
  597.0 4.9 custom-call.15
  602.3 2.1 fusion.59
  604.5 9.4 %all_to_all.34 = f32[64,8,128]{2,1,0:T(8,128)S(1)} all-to-all(f32[64,8,128]{2,1,0:T(8,128)S(1)} %copy.19), channel_id=1, replica_groups=mesh['af'=4,'ga'=8,'ha'=16] {'af'}, dimensions={0} | all-to-all | bytes 524288 | tf_op jit(solution)/shard_map/all_to_all | solution.py:34
  614.0 0.7 copy.26
  (46 shorter events, 9.0 us)
Async XLA Ops:
  6.5 510.6 %copy-start = (f32[512,64]{0,1:T(8,128)S(1)}, f32[512,64]{0,1:T(8,128)}, u32[]{:S(2)}) copy-start(f32[512,64]{0,1:T(8,128)} %param.6) | copy-start | bytes 393220
  6.5 510.6 %all-reduce.2.cloned.1.call-start = ((), (), s32[]{:S(2)}) async-start(), calls=%async_computation.2 | async-start | bytes 2097152 | tf_op jit(solution)/shard_map/psum | solution.py:28
  37.2 4.5 copy-start.2
  517.1 15.3 %copy-start.1 = (f32[512,512]{1,0:T(8,128)S(1)}, f32[512,512]{1,0:T(8,128)}, u32[]{:S(2)}) copy-start(f32[512,512]{1,0:T(8,128)} %all-reduce.2.cloned.1.call-done) | copy-start | bytes 3145732
Sparse Core Ops, SparseCore 0:
  41.9 475.1 all-reduce.1
where the time goes:
time: 622 us
  waiting for transfers between devices  474 us (76%)
  other arithmetic  72.6 us (12%)
  blocking collectives  35.2 us (6%)
  matrix products  18.5 us (3%)
  between operations  13.7 us (2%)
  local copies, waits for them, and re-layouts  8 us (1%)
    psum x1, waiting for transfers between devices, per_device(): gram = lax.psum(partial_gram, ('af', 'ga', 'ha')) * (1.0 / ncols)  474 us
    another operation x18, other arithmetic, orthonormal(): lower = jnp.linalg.cholesky(inner)  39.2 us
    another operation x12, other arithmetic, orthonormal(): lax.linalg.triangular_solve(lower, work, left_side=False, lower=True, tra...  33.3 us
    all_to_all x1, blocking collectives, per_device(): lax.all_to_all(field, 'af', split_axis=1, concat_axis=0, tiled=True)  25.8 us
  transfers between devices with their start and end apart: 1, of which 1 were waited for; matrix products, arithmetic and copies ran while one was open for 0% of the time, Pallas kernels for 0%

commit v1 on v0

v1 whole, which is shorter than its diff:
```python
import functools

import jax
import jax.numpy as jnp
from jax import lax
from jax.experimental import pallas as pl
from jax.experimental.pallas import tpu as pltpu
from jax.sharding import PartitionSpec as P

ITERS = 6
HIGHEST = lax.Precision.HIGHEST
MESH = pl.DeviceIdType.MESH
VMEM_LIMIT = 56 * 2**20


def dot_nt(a, b):
    dims = (((1,), (1,)), ((), ()))
    return lax.dot_general(a, b, dims, precision=HIGHEST, preferred_element_type=jnp.float32)


def dot(a, b):
    return jnp.dot(a, b, precision=HIGHEST, preferred_element_type=jnp.float32)


def chol_inverse(inner):
    n = inner.shape[0]
    width = 2 * n
    panels = n // 8
    sub = lax.broadcasted_iota(jnp.int32, (8, width), 0)
    lane = lax.broadcasted_iota(jnp.int32, (8, n), 1)
    subn = lax.broadcasted_iota(jnp.int32, (8, n), 0)
    rows = []
    for m in range(panels):
        eye = jnp.where(lane == subn + 8 * m, 1.0, 0.0).astype(jnp.float32)
        rows.append(jnp.concatenate([inner[8 * m:8 * m + 8, :], eye], axis=1))
    full = (8, width)
    out = []
    for k in range(panels):
        cols = {m: [jnp.broadcast_to(rows[m][:, 8 * k + p:8 * k + p + 1], full) for p in range(8)] for m in range(k, panels)}
        D = {}
        for p in range(8):
            for q in range(p, 8):
                D[q, p] = jnp.broadcast_to(cols[k][p][q:q + 1, :], full)
        row = [jnp.broadcast_to(rows[k][p:p + 1, :], full) for p in range(8)]
        dinv = []
        for p in range(8):
            dinv.append(1.0 / D[p, p])
            for q in range(p + 1, 8):
                f = D[q, p] * dinv[p]
                for r in range(p + 1, q + 1):
                    D[q, r] = D[q, r] - f * D[r, p]
                row[q] = row[q] - f * row[p]
                for m in range(k + 1, panels):
                    cols[m][q] = cols[m][q] - f * cols[m][p]
        for m in range(k + 1, panels):
            acc = rows[m]
            for p in range(8):
                acc = acc - (cols[m][p] * dinv[p]) * row[p]
            rows[m] = acc
        res = row[0] * lax.rsqrt(D[0, 0])
        for p in range(1, 8):
            res = jnp.where(sub == p, row[p] * lax.rsqrt(D[p, p]), res)
        out.append(res[:, n:])
    return jnp.concatenate(out, axis=0)


def iterate_kernel(iters, scale, s_ref, start_ref, out_ref, g_ref, w_ref):
    for p in range(4):
        blk = s_ref[pl.ds(128 * p, 128), :] * scale
        g_ref[128 * p:128 * p + 128, 128 * p:128 * p + 128] = blk
        q = (p + 1) % 4
        blk = s_ref[pl.ds(512 + 128 * p, 128), :] * scale
        g_ref[128 * p:128 * p + 128, 128 * q:128 * q + 128] = blk
        g_ref[128 * q:128 * q + 128, 128 * p:128 * p + 128] = blk.T
    for p in range(2):
        q = p + 2
        blk = s_ref[pl.ds(1024 + 128 * p, 128), :] * scale
        g_ref[128 * p:128 * p + 128, 128 * q:128 * q + 128] = blk
        g_ref[128 * q:128 * q + 128, 128 * p:128 * p + 128] = blk.T
    w_ref[...] = dot(start_ref[...].T, g_ref[...])

    def step(i, carry):
        work = w_ref[...]
        linv = chol_inverse(dot_nt(work, work))
        ahead = dot(work, g_ref[...])
        w_ref[...] = dot(linv, ahead)
        return carry
    lax.fori_loop(0, iters - 1, step, 0)
    work = w_ref[...]
    linv = chol_inverse(dot_nt(work, work))
    out_ref[...] = dot(linv, work)


def iterate(s, start, iters, scale):
    n, r = start.shape
    return pl.pallas_call(
        functools.partial(iterate_kernel, iters, scale),
        out_shape=jax.ShapeDtypeStruct((r, n), jnp.float32),
        in_specs=[pl.BlockSpec(memory_space=pltpu.VMEM)] * 2,
        out_specs=pl.BlockSpec(memory_space=pltpu.VMEM),
        scratch_shapes=[pltpu.VMEM((n, n), jnp.float32), pltpu.VMEM((r, n), jnp.float32)],
        compiler_params=pltpu.CompilerParams(vmem_limit_bytes=VMEM_LIMIT),
        name="iterate",
    )(s, start)


def gram_kernel(field_ref, cols_ref, gram_ref, half, near, acc, slots, quad, fours, full,
                in_send, in_recv, own_sem, core_send, core_recv, plane_send, plane_recv,
                z_send, z_recv, out_send, out_recv):
    x, g, z = lax.axis_index("af"), lax.axis_index("ga"), lax.axis_index("ha")
    core = lax.rem(g, 2)
    y = g // 2
    rows = field_ref.shape[0]
    parts = 4
    chunk = rows // parts

    def at(dx, dg, dz):
        return {"af": lax.rem(x + dx, 4), "ga": lax.rem(g + dg, 8), "ha": lax.rem(z + dz, 16)}

    other_core = {"af": x, "ga": g + 1 - 2 * core, "ha": z}
    plane = [(a, b) for a in range(4) for b in range(4) if (a, b) != (0, 0)]

    barrier = pltpu.get_barrier_semaphore()
    partners = [at(0, 0, d) for d in (4, 8, 12, 1, 2, 15, 14)]
    partners += [at(a, 2 * b, 0) for a, b in plane] + [other_core]
    for device in partners:
        pl.semaphore_signal(barrier, inc=1, device_id=device, device_id_type=MESH)
    pl.semaphore_wait(barrier, len(partners))

    sends = []
    for c in range(parts):
        for k, d in enumerate((1, 3, 2)):
            to = lax.rem(x + d, 4)
            copy = pltpu.make_async_remote_copy(
                src_ref=field_ref.at[pl.ds(c * chunk, chunk), pl.ds(to * 8, 8), :],
                dst_ref=cols_ref.at[pl.ds(x * rows + c * chunk, chunk)],
                send_sem=in_send.at[k, c],
                recv_sem=in_recv.at[k, c],
                device_id=at(d, 0, 0),
                device_id_type=MESH,
            )
            copy.start()
            sends.append(copy)
    own = pltpu.make_async_copy(
        field_ref.at[:, pl.ds(x * 8, 8), :], cols_ref.at[pl.ds(x * rows, rows)], own_sem
    )
    own.start()

    def arrived(k, d):
        for c in range(parts):
            source = lax.rem(x + 4 - d, 4)
            landing = cols_ref.at[pl.ds(source * rows + c * chunk, chunk)]
            pltpu.make_async_remote_copy(
                src_ref=landing, dst_ref=landing, send_sem=in_send.at[k, c],
                recv_sem=in_recv.at[k, c], device_id=at(d, 0, 0), device_id_type=MESH,
            ).wait_recv()

    flat = cols_ref.reshape(4 * rows * 8, 128)

    def block(p, q, slot):
        total = jnp.zeros((rows, rows), jnp.float32)
        for s in range(0, 8, 2):
            left = [flat[pl.ds(p * rows * 8 + s + t, rows, stride=8), :] for t in range(2)]
            right = [flat[pl.ds(q * rows * 8 + s + t, rows, stride=8), :] for t in range(2)]
            total += dot_nt(jnp.concatenate(left, axis=1), jnp.concatenate(right, axis=1))
        half[pl.ds(slot * rows, rows), :] = total

    after, opposite, before = (lax.rem(x + d, 4) for d in (1, 2, 3))
    own.wait()
    block(x, x, x)
    arrived(1, 3)
    block(x, after, 4 + x)
    block(after, after, after)
    arrived(0, 1)
    block(before, x, 4 + before)
    block(before, before, before)
    pair = lax.rem(after, 2)
    block(pair, pair + 2, 8 + pair)
    arrived(2, 2)
    block(after, opposite, 4 + after)
    block(opposite, before, 4 + opposite)
    block(opposite, opposite, opposite)
    pair = lax.rem(x, 2)
    block(pair, pair + 2, 8 + pair)

    count = half.shape[0] // 2
    mine = pl.ds(core * count, count)
    swap = pltpu.make_async_remote_copy(
        src_ref=half.at[pl.ds((1 - core) * count, count)], dst_ref=near,
        send_sem=core_send.at[0], recv_sem=core_recv.at[0],
        device_id=other_core, device_id_type=MESH,
    )
    swap.start()
    swap.wait_recv()
    sends.append(swap)
    acc[...] = half[mine, :] + near[...]

    size = count // 16
    me = x * 4 + y
    for i, (a, b) in enumerate(plane):
        to = lax.rem(x + a, 4) * 4 + lax.rem(y + b, 4)
        copy = pltpu.make_async_remote_copy(
            src_ref=acc.at[pl.ds(to * size, size)], dst_ref=slots.at[me],
            send_sem=plane_send.at[i], recv_sem=plane_recv.at[i],
            device_id=at(a, 2 * b, 0), device_id_type=MESH,
        )
        copy.start()
        sends.append(copy)
    slots[me] = acc[pl.ds(me * size, size), :]
    for copy in sends[-15:]:
        copy.wait_recv()
    zq, zr = z // 4, lax.rem(z, 4)
    total = slots[0]
    for i in range(1, 16):
        total += slots[i]
    quad[zq] = total

    for i, d in enumerate((4, 8, 12)):
        copy = pltpu.make_async_remote_copy(
            src_ref=quad.at[zq], dst_ref=quad.at[zq], send_sem=z_send.at[i],
            recv_sem=z_recv.at[i], device_id=at(0, 0, d), device_id_type=MESH,
        )
        copy.start()
        sends.append(copy)
    for copy in sends[-3:]:
        copy.wait_recv()
    fours[zr] = ((quad[0] + quad[1]) + quad[2]) + quad[3]
    for i, d in enumerate((1, 15, 2)):
        copy = pltpu.make_async_remote_copy(
            src_ref=fours.at[zr], dst_ref=fours.at[zr], send_sem=z_send.at[3 + i],
            recv_sem=z_recv.at[3 + i], device_id=at(0, 0, d), device_id_type=MESH,
        )
        copy.start()
        sends.append(copy)
    for copy in sends[-3:]:
        copy.wait_recv()
    total = ((fours[0] + fours[1]) + fours[2]) + fours[3]

    here = pl.ds(core * count + me * size, size)
    full[here, :] = total
    for i, (a, b) in enumerate(plane):
        copy = pltpu.make_async_remote_copy(
            src_ref=full.at[here], dst_ref=full.at[here],
            send_sem=out_send.at[i], recv_sem=out_recv.at[i],
            device_id=at(a, 2 * b, 0), device_id_type=MESH,
        )
        copy.start()
        sends.append(copy)
    for copy in sends[-15:]:
        copy.wait_recv()
    swap = pltpu.make_async_remote_copy(
        src_ref=full.at[mine], dst_ref=full.at[mine],
        send_sem=core_send.at[1], recv_sem=core_recv.at[1],
        device_id=other_core, device_id_type=MESH,
    )
    swap.start()
    swap.wait_recv()
    sends.append(swap)
    gram_ref[...] = full[...]
    for copy in sends:
        copy.wait_send()


def gram_blocks(field):
    rows = field.shape[0]
    dma = pltpu.SemaphoreType.DMA
    vmem = pltpu.VMEM
    return pl.pallas_call(
        gram_kernel,
        out_shape=(
            jax.ShapeDtypeStruct((4 * rows, 8, 128), jnp.float32),
            jax.ShapeDtypeStruct((10 * rows, rows), jnp.float32),
        ),
        in_specs=[pl.BlockSpec(memory_space=pl.ANY)],
        out_specs=(pl.BlockSpec(memory_space=vmem), pl.BlockSpec(memory_space=vmem)),
        scratch_shapes=[
            vmem((10 * rows, rows), jnp.float32),
            vmem((5 * rows, rows), jnp.float32),
            vmem((5 * rows, rows), jnp.float32),
            vmem((16, 5 * rows // 16, rows), jnp.float32),
            vmem((4, 5 * rows // 16, rows), jnp.float32),
            vmem((4, 5 * rows // 16, rows), jnp.float32),
            vmem((10 * rows, rows), jnp.float32),
            dma((3, 4)), dma((3, 4)), dma(()), dma((2,)), dma((2,)), dma((15,)), dma((15,)),
            dma((6,)), dma((6,)), dma((15,)), dma((15,)),
        ],
        compiler_params=pltpu.CompilerParams(
            collective_id=0, has_side_effects=True, vmem_limit_bytes=VMEM_LIMIT
        ),
        name="gram_blocks",
    )(field)


def project_kernel(cols_ref, basis_ref, out_ref, proj, stage, send_sem, recv_sem):
    x = lax.axis_index("af")

    def at(d):
        return {"af": lax.rem(x + d, 4)}

    barrier = pltpu.get_barrier_semaphore()
    for d in (1, 2, 3):
        pl.semaphore_signal(barrier, inc=1, device_id=at(d), device_id_type=MESH)
    ranks, total_rows = basis_ref.shape
    flat = cols_ref.reshape(total_rows * 8, 128)
    flat_out = proj.reshape(ranks * 8, 128)
    basis = basis_ref[...]
    for s in range(0, 8, 2):
        pieces = [flat[pl.ds(s + t, total_rows, stride=8), :] for t in range(2)]
        part = dot(basis, jnp.concatenate(pieces, axis=1))
        for t in range(2):
            flat_out[pl.ds(s + t, ranks, stride=8), :] = part[:, 128 * t:128 * t + 128]
    pl.semaphore_wait(barrier, 3)
    share = ranks // 4
    copies = []
    for k, d in enumerate((2, 1, 3)):
        to = lax.rem(x + d, 4)
        copy = pltpu.make_async_remote_copy(
            src_ref=proj.at[pl.ds(to * share, share)],
            dst_ref=stage.at[:, pl.ds(x * 8, 8), :],
            send_sem=send_sem.at[k], recv_sem=recv_sem.at[k],
            device_id=at(d), device_id_type=MESH,
        )
        copy.start()
        copies.append(copy)
    stage[:, pl.ds(x * 8, 8), :] = proj[pl.ds(x * share, share)]
    for copy in copies:
        copy.wait_recv()
    out_ref[...] = stage[...]
    for copy in copies:
        copy.wait_send()


def project(cols, basis):
    ranks = basis.shape[0]
    dma = pltpu.SemaphoreType.DMA
    vmem = pltpu.VMEM
    return pl.pallas_call(
        project_kernel,
        out_shape=jax.ShapeDtypeStruct((ranks // 4, 32, 128), jnp.float32),
        in_specs=[pl.BlockSpec(memory_space=vmem)] * 2,
        out_specs=pl.BlockSpec(memory_space=vmem),
        scratch_shapes=[
            vmem((ranks, 8, 128), jnp.float32),
            vmem((ranks // 4, 32, 128), jnp.float32),
            dma((3,)), dma((3,)),
        ],
        compiler_params=pltpu.CompilerParams(
            collective_id=1, has_side_effects=True, vmem_limit_bytes=VMEM_LIMIT
        ),
        name="project",
    )(cols, basis)


def per_device(field, start):
    ncols = field.shape[1] * field.shape[2] * lax.axis_size("ga") * lax.axis_size("ha")
    cols, blocks = gram_blocks(field)
    basis = iterate(blocks, start, ITERS, 1.0 / ncols)
    return project(cols, basis)


def solution(mesh):
    placed = (P("af", "ga", "ha"), P())
    return jax.shard_map(
        per_device, mesh=mesh, in_specs=placed, out_specs=P("af", "ga", "ha"), check_vma=False
    )
```

time: 622 us -> 106 us (0.17)
  waiting for transfers between devices: 474 us -> 0 us
  Pallas kernels: 0 us -> 103 us
  other arithmetic: 72.6 us -> 0 us
  blocking collectives: 35.2 us -> 0 us
  matrix products: 18.5 us -> 0 us
  between operations: 13.7 us -> 0.03 us
    psum x1 -> x0, waiting for transfers between devices: 474 us -> none  [per_device(): gram = lax.psum(partial_gram, ('af', 'ga', 'ha')) * (1.0 / ncols)]
    pallas_call x0 -> x3, Pallas kernels: none -> 103 us  [the longest x1 75.1 us: gram_blocks(): pl.pallas_call(gram_kernel, out_shape=(jax.ShapeDtypeStruct((4 * rows, 8,...]
    another operation x30 -> x0, other arithmetic: 72.5 us -> none  [the longest x18 39.2 us: orthonormal(): lower = jnp.linalg.cholesky(inner)]
    all_to_all x2 -> x0, blocking collectives: 35.2 us -> none  [the longest x1 25.8 us: per_device(): lax.all_to_all(field, 'af', split_axis=1, concat_axis=0, tiled=True)]
    dot_general x14 -> x0, matrix products: 16.5 us -> none  [the longest x6 8.28 us: per_device(): jnp.dot(gram, basis, precision=highest, preferred_element_type=jnp.float32)]
  transfers between devices with their start and end apart: 1 -> 0, of which waited for: 1 -> 0; matrix products, arithmetic and copies ran while one was open for 0% -> 0% of each run, Pallas kernels for 0% -> 0%
where the time goes in v1:
time: 106 us
  Pallas kernels  103 us (97%)
  local copies, waits for them, and re-layouts  2.51 us (2%)
    pallas_call x1, Pallas kernels, gram_blocks(): pl.pallas_call(gram_kernel, out_shape=(jax.ShapeDtypeStruct((4 * rows, 8,...  75.1 us
    pallas_call x1, Pallas kernels, iterate(): pl.pallas_call(functools.partial(iterate_kernel, iters, scale), out_shape...  18.5 us
    pallas_call x1, Pallas kernels, project(): pl.pallas_call(project_kernel, out_shape=jax.ShapeDtypeStruct((ranks // 4...  9.58 us
    unnamed x4, local copies, waits for them, and re-layouts  2.51 us

profile of v1, /device:TPU:1, one launch (start us, length us, event | category | flops | bytes accessed | tf_op | source)
XLA Modules:
  0.0 105.7 jit_solution(15660942827970363210)
XLA Ops:
  0.0 0.0 copy-start
  0.0 75.1 %gram_blocks.1 = (f32[512,8,128]{2,1,0:T(8,128)}, f32[1280,128]{1,0:T(8,128)}) custom-call(f32[128,32,128]{2,1,0:T(8,128)} %field_ref.1), custom_call_target="tpu_custom_call" | custom-call | tf_op jit(solution)/shard_map/gram_blocks/pallas_call | solution.py:268
  75.1 0.0 copy-done
  75.1 0.8 copy.3.start_ref
  76.0 18.5 %iterate.1.basis_ref = f32[64,512]{1,0:T(8,128)} custom-call(f32[1280,128]{1,0:T(8,128)} %get-tuple-element.8.s_ref, f32[512,64]{1,0:T(8,128)} %copy.3.start_ref), custom_call_target="tpu_custom_call" | custom-call | tf_op jit(solution)/shard_map/iterate/pallas_call | solution.py:96
  94.4 9.6 %project.1 = f32[16,32,128]{2,1,0:T(8,128)} custom-call(f32[512,8,128]{2,1,0:T(8,128)} %get-tuple-element.7.cols_ref, f32[64,512]{1,0:T(8,128)} %iterate.1.basis_ref), custom_call_target="tpu_custom_call" | custom-call | tf_op jit(solution)/shard_map/project/pallas_call | solution.py:337
  104.0 1.7 %copy.5 = f32[16,32,128]{2,1,0:T(8,128)} copy(f32[16,32,128]{2,1,0:T(8,128)} %project.1) | data formatting | bytes 524288
Async XLA Ops:
  0.0 75.1 %copy-start = (f32[512,64]{0,1:T(8,128)S(1)}, f32[512,64]{0,1:T(8,128)}, u32[]{:S(2)}) copy-start(f32[512,64]{0,1:T(8,128)} %param.3) | copy-start | bytes 393220

commit v2 on v0

v2 whole, which is shorter than its diff:
```python
import functools

import jax
import jax.numpy as jnp
from jax import lax
from jax.experimental import pallas as pl
from jax.experimental.pallas import tpu as pltpu
from jax.sharding import PartitionSpec as P

ITERS = 6
HIGHEST = lax.Precision.HIGHEST
MESH = pl.DeviceIdType.MESH
NT = (((1,), (1,)), ((), ()))
VMEM_LIMIT = 56 * 2**20


def dot(a, b):
    return jnp.dot(a, b, precision=HIGHEST, preferred_element_type=jnp.float32)


def dot_nt(a, b):
    return lax.dot_general(a, b, NT, precision=HIGHEST, preferred_element_type=jnp.float32)


def dot16(a, b):
    return jnp.dot(a, b, preferred_element_type=jnp.float32)


def dot16_nt(a, b):
    return lax.dot_general(a, b, NT, preferred_element_type=jnp.float32)


def split(x):
    high = x.astype(jnp.bfloat16)
    rest = x - high.astype(jnp.float32)
    mid = rest.astype(jnp.bfloat16)
    low = (rest - mid.astype(jnp.float32)).astype(jnp.bfloat16)
    return high, mid, low


def chol_inverse(inner):
    n = inner.shape[0]
    width = 2 * n
    panels = n // 8
    sub = lax.broadcasted_iota(jnp.int32, (8, width), 0)
    lane = lax.broadcasted_iota(jnp.int32, (8, n), 1)
    subn = lax.broadcasted_iota(jnp.int32, (8, n), 0)
    rows = []
    for m in range(panels):
        eye = jnp.where(lane == subn + 8 * m, 1.0, 0.0).astype(jnp.float32)
        rows.append(jnp.concatenate([inner[8 * m:8 * m + 8, :], eye], axis=1))
    full = (8, width)
    out = []
    for k in range(panels):
        cols = {m: [jnp.broadcast_to(rows[m][:, 8 * k + p:8 * k + p + 1], full) for p in range(8)] for m in range(k, panels)}
        D = {}
        for p in range(8):
            for q in range(p, 8):
                D[q, p] = jnp.broadcast_to(cols[k][p][q:q + 1, :], full)
        row = [jnp.broadcast_to(rows[k][p:p + 1, :], full) for p in range(8)]
        dinv = []
        for p in range(8):
            dinv.append(1.0 / D[p, p])
            for q in range(p + 1, 8):
                f = D[q, p] * dinv[p]
                for r in range(p + 1, q + 1):
                    D[q, r] = D[q, r] - f * D[r, p]
                row[q] = row[q] - f * row[p]
                for m in range(k + 1, panels):
                    cols[m][q] = cols[m][q] - f * cols[m][p]
        for m in range(k + 1, panels):
            acc = rows[m]
            for p in range(8):
                acc = acc - (cols[m][p] * dinv[p]) * row[p]
            rows[m] = acc
        res = row[0] * lax.rsqrt(D[0, 0])
        for p in range(1, 8):
            res = jnp.where(sub == p, row[p] * lax.rsqrt(D[p, p]), res)
        out.append(res[:, n:])
    return jnp.concatenate(out, axis=0)


def step_kernel(iters, scale, field_ref, start_ref, out_ref, cols, high, mid, low, half, near, acc,
                slots, quad, fours, full, gram, work_ref, proj, stage, in_send, in_recv, own_sem,
                core_send, core_recv, plane_send, plane_recv, z_send, z_recv, back_send, back_recv,
                out_send, out_recv, met):
    x, g, z = lax.axis_index("af"), lax.axis_index("ga"), lax.axis_index("ha")
    core = lax.rem(g, 2)
    y = g // 2
    rows = field_ref.shape[0]

    def at(dx, dg, dz):
        return {"af": lax.rem(x + dx, 4), "ga": lax.rem(g + dg, 8), "ha": lax.rem(z + dz, 16)}

    other_core = {"af": x, "ga": g + 1 - 2 * core, "ha": z}
    plane = [(a, b) for a in range(4) for b in range(4) if (a, b) != (0, 0)]
    sends = []

    def send(src, dst, send_sem, recv_sem, device):
        copy = pltpu.make_async_remote_copy(
            src_ref=src, dst_ref=dst, send_sem=send_sem, recv_sem=recv_sem,
            device_id=device, device_id_type=MESH,
        )
        copy.start()
        sends.append(copy)
        return copy

    barrier = pltpu.get_barrier_semaphore()
    nearest = [at(1, 0, 0), at(3, 0, 0), at(2, 0, 0), other_core]
    nearest += [at(0, 2, 0), at(0, 6, 0), at(0, 0, 1), at(0, 0, 15)]
    for device in nearest:
        pl.semaphore_signal(barrier, inc=1, device_id=device, device_id_type=MESH)
    pl.semaphore_wait(barrier, len(nearest))

    for k, d in enumerate((1, 3, 2)):
        send(
            field_ref.at[:, pl.ds(lax.rem(x + d, 4) * 8, 8), :], cols.at[pl.ds(x * rows, rows)],
            in_send.at[k], in_recv.at[k], at(d, 0, 0),
        )
    incoming = {d: sends[k] for k, d in enumerate((3, 1, 2))}
    own = pltpu.make_async_copy(
        field_ref.at[:, pl.ds(x * 8, 8), :], cols.at[pl.ds(x * rows, rows)], own_sem
    )
    own.start()

    rounds = (
        (at(0, 2, 0), at(0, 6, 0), at(0, 0, 1), at(0, 0, 15)),
        (at(0, 4, 0), at(0, 0, 2), at(0, 0, 14)),
        (at(0, 0, 4), at(0, 0, 12)),
    )
    index = 0
    for devices in rounds:
        for i, device in enumerate(devices):
            pl.semaphore_signal(met.at[index + i], inc=1, device_id=device, device_id_type=MESH)
        for i in range(len(devices)):
            pl.semaphore_wait(met.at[index + i], 1)
        index += len(devices)

    flat = cols.reshape(4 * rows * 8, 128)

    def ready(p):
        for s in range(8):
            parts = split(flat[pl.ds(p * rows * 8 + s, rows, stride=8), :])
            for ref, part in zip((high, mid, low), parts):
                ref[pl.ds(p * rows, rows), 128 * s:128 * s + 128] = part

    def block(p, q, slot):
        left, right = pl.ds(p * rows, rows), pl.ds(q * rows, rows)
        main = dot16_nt(
            jnp.concatenate([high[left, :], mid[left, :]], axis=0),
            jnp.concatenate([high[right, :], mid[right, :]], axis=0),
        )
        small = dot16_nt(low[left, :], high[right, :]) + dot16_nt(high[left, :], low[right, :])
        small += main[rows:, rows:]
        half[pl.ds(slot * rows, rows), :] = main[:rows, :rows] + (
            (main[:rows, rows:] + main[rows:, :rows]) + small
        )

    after, opposite, before = (lax.rem(x + d, 4) for d in (1, 2, 3))
    own.wait()
    ready(x)
    block(x, x, x)
    incoming[1].wait_recv()
    ready(after)
    block(x, after, 4 + x)
    block(after, after, after)
    incoming[3].wait_recv()
    ready(before)
    block(before, x, 4 + before)
    block(before, before, before)
    pair = lax.rem(after, 2)
    block(pair, pair + 2, 8 + pair)
    incoming[2].wait_recv()
    ready(opposite)
    block(after, opposite, 4 + after)
    block(opposite, before, 4 + opposite)
    block(opposite, opposite, opposite)
    pair = lax.rem(x, 2)
    block(pair, pair + 2, 8 + pair)

    count = half.shape[0] // 2
    mine = pl.ds(core * count, count)
    send(
        half.at[pl.ds((1 - core) * count, count)], near, core_send.at[0], core_recv.at[0], other_core
    ).wait_recv()
    acc[...] = half[mine, :] + near[...]

    size = count // 16
    me = x * 4 + y
    arrivals = []
    for i, (a, b) in enumerate(plane):
        to = lax.rem(x + a, 4) * 4 + lax.rem(y + b, 4)
        arrivals.append(send(
            acc.at[pl.ds(to * size, size)], slots.at[me],
            plane_send.at[i], plane_recv.at[i], at(a, 2 * b, 0),
        ))
    slots[me] = acc[pl.ds(me * size, size), :]
    for copy in arrivals:
        copy.wait_recv()
    zq, zr = z // 4, lax.rem(z, 4)
    total = slots[0]
    for i in range(1, 16):
        total += slots[i]

    for index, (ref, own_slot, steps) in enumerate(((quad, zq, (8, 4, 12)), (fours, zr, (2, 1, 15)))):
        ref[own_slot] = total
        arrivals = [
            send(
                ref.at[own_slot], ref.at[own_slot],
                z_send.at[3 * index + i], z_recv.at[3 * index + i], at(0, 0, d),
            )
            for i, d in enumerate(steps)
        ]
        for copy in arrivals:
            copy.wait_recv()
        total = ((ref[0] + ref[1]) + ref[2]) + ref[3]

    here = pl.ds(core * count + me * size, size)
    full[here, :] = total
    arrivals = [
        send(full.at[here], full.at[here], back_send.at[i], back_recv.at[i], at(a, 2 * b, 0))
        for i, (a, b) in enumerate(plane)
    ]
    for copy in arrivals:
        copy.wait_recv()
    send(
        full.at[mine], full.at[mine], core_send.at[1], core_recv.at[1], other_core
    ).wait_recv()
    for p in range(4):
        q = (p + 1) % 4
        gram[rows * p:rows * p + rows, rows * p:rows * p + rows] = (
            full[rows * p:rows * p + rows, :] * scale
        )
        pairs = [(p, q, 4 + p)] + ([(p, p + 2, 8 + p)] if p < 2 else [])
        for a, b, slot in pairs:
            part = full[rows * slot:rows * slot + rows, :] * scale
            gram[rows * a:rows * a + rows, rows * b:rows * b + rows] = part
            gram[rows * b:rows * b + rows, rows * a:rows * a + rows] = part.T

    work_ref[...] = dot(start_ref[...], gram[...])

    def step(i, carry):
        work = work_ref[...]
        inverse = chol_inverse(dot_nt(work, work))
        ahead = dot(work, gram[...])
        work_ref[...] = dot(inverse, jnp.where(i < iters - 1, ahead, work))
        return carry

    lax.fori_loop(0, iters, step, 0)

    parts = split(work_ref[...])
    ranks = work_ref.shape[0]
    main = dot16(jnp.concatenate(parts, axis=0), high[...])
    middle = dot16(jnp.concatenate(parts[:2], axis=0), mid[...])
    small = dot16(parts[0], low[...])
    result = main[:ranks] + (
        (main[ranks:2 * ranks] + middle[:ranks]) + (middle[ranks:] + (main[2 * ranks:] + small))
    )
    flat_out = proj.reshape(ranks * 8, 128)
    for s in range(8):
        flat_out[pl.ds(s, ranks, stride=8), :] = result[:, 128 * s:128 * s + 128]
    share = ranks // 4
    arrivals = [
        send(
            proj.at[pl.ds(lax.rem(x + d, 4) * share, share)], stage.at[:, pl.ds(x * 8, 8), :],
            out_send.at[k], out_recv.at[k], at(d, 0, 0),
        )
        for k, d in enumerate((2, 1, 3))
    ]
    stage[:, pl.ds(x * 8, 8), :] = proj[pl.ds(x * share, share)]
    for copy in arrivals:
        copy.wait_recv()
    out_ref[...] = stage[...]
    for copy in sends:
        copy.wait_send()


def per_device(field, start):
    ncols = field.shape[1] * field.shape[2] * lax.axis_size("ga") * lax.axis_size("ha")
    rows = field.shape[0]
    total, ranks = start.shape
    dma, vmem, f32 = pltpu.SemaphoreType.DMA, pltpu.VMEM, jnp.float32
    piece = 5 * rows // 16
    return pl.pallas_call(
        functools.partial(step_kernel, ITERS, 1.0 / ncols),
        out_shape=jax.ShapeDtypeStruct((ranks // 4, 32, 128), f32),
        in_specs=[pl.BlockSpec(memory_space=pl.ANY), pl.BlockSpec(memory_space=vmem)],
        out_specs=pl.BlockSpec(memory_space=vmem),
        scratch_shapes=[
            vmem((total, 8, 128), f32),
            vmem((total, 1024), jnp.bfloat16),
            vmem((total, 1024), jnp.bfloat16),
            vmem((total, 1024), jnp.bfloat16),
            vmem((10 * rows, rows), f32),
            vmem((5 * rows, rows), f32),
            vmem((5 * rows, rows), f32),
            vmem((16, piece, rows), f32),
            vmem((4, piece, rows), f32),
            vmem((4, piece, rows), f32),
            vmem((10 * rows, rows), f32),
            vmem((total, total), f32),
            vmem((ranks, total), f32),
            vmem((ranks, 8, 128), f32),
            vmem((ranks // 4, 32, 128), f32),
            dma((3,)), dma((3,)), dma(()), dma((2,)), dma((2,)), dma((15,)), dma((15,)),
            dma((6,)), dma((6,)), dma((15,)), dma((15,)), dma((3,)), dma((3,)),
            pltpu.SemaphoreType.REGULAR((9,)),
        ],
        compiler_params=pltpu.CompilerParams(
            collective_id=0, has_side_effects=True, vmem_limit_bytes=VMEM_LIMIT
        ),
        name="hosvd_step",
    )(field, start.T)


def solution(mesh):
    placed = (P("af", "ga", "ha"), P())
    return jax.shard_map(
        per_device, mesh=mesh, in_specs=placed, out_specs=P("af", "ga", "ha"), check_vma=False
    )
```

time: 622 us -> 93.4 us (0.15)
  waiting for transfers between devices: 474 us -> 0 us
  Pallas kernels: 0 us -> 91.5 us
  other arithmetic: 72.6 us -> 0 us
  blocking collectives: 35.2 us -> 0 us
  matrix products: 18.5 us -> 0 us
  between operations: 13.7 us -> 0.01 us
  local copies, waits for them, and re-layouts: 8 us -> 1.67 us
    psum x1 -> x0, waiting for transfers between devices: 474 us -> none  [per_device(): gram = lax.psum(partial_gram, ('af', 'ga', 'ha')) * (1.0 / ncols)]
    pallas_call x0 -> x1, Pallas kernels: none -> 91.5 us  [per_device(): pl.pallas_call(functools.partial(step_kernel, ITERS, 1.0 / ncols), out_sh...]
    another operation x30 -> x0, other arithmetic: 72.5 us -> none  [the longest x18 39.2 us: orthonormal(): lower = jnp.linalg.cholesky(inner)]
    all_to_all x2 -> x0, blocking collectives: 35.2 us -> none  [the longest x1 25.8 us: per_device(): lax.all_to_all(field, 'af', split_axis=1, concat_axis=0, tiled=True)]
    dot_general x14 -> x0, matrix products: 16.5 us -> none  [the longest x6 8.28 us: per_device(): jnp.dot(gram, basis, precision=highest, preferred_element_type=jnp.float32)]
  transfers between devices with their start and end apart: 1 -> 0, of which waited for: 1 -> 0; matrix products, arithmetic and copies ran while one was open for 0% -> 0% of each run, Pallas kernels for 0% -> 0%
where the time goes in v2:
time: 93.4 us; the launch traced here: 93.2 us
  Pallas kernels  91.5 us (98%)
  local copies, waits for them, and re-layouts  1.67 us (2%)
    pallas_call x1, Pallas kernels, per_device(): pl.pallas_call(functools.partial(step_kernel, ITERS, 1.0 / ncols), out_sh...  91.5 us

profile of v2, /device:TPU:1, one launch (start us, length us, event | category | flops | bytes accessed | tf_op | source)
XLA Modules:
  0.0 93.2 jit_solution(1345788055039607588)
XLA Ops:
  0.0 91.5 %hosvd_step.1 = f32[16,32,128]{2,1,0:T(8,128)} custom-call(f32[128,32,128]{2,1,0:T(8,128)} %field_ref.1, f32[64,512]{1,0:T(8,128)} %bitcast.1), custom_call_target="tpu_custom_call" | custom-call | tf_op jit(solution)/shard_map/hosvd_step/pallas_call | solution.py:284
  91.5 1.7 %copy.4 = f32[16,32,128]{2,1,0:T(8,128)} copy(f32[16,32,128]{2,1,0:T(8,128)} %hosvd_step.1) | data formatting | bytes 524288

commit v3 on v2

--- a/solution.py
+++ b/solution.py
@@ -40,48 +40,70 @@
 
 def chol_inverse(inner):
     n = inner.shape[0]
-    width = 2 * n
     panels = n // 8
-    sub = lax.broadcasted_iota(jnp.int32, (8, width), 0)
+    full = (8, 2 * n)
+    sub = lax.broadcasted_iota(jnp.int32, full, 0)
     lane = lax.broadcasted_iota(jnp.int32, (8, n), 1)
-    subn = lax.broadcasted_iota(jnp.int32, (8, n), 0)
     rows = []
     for m in range(panels):
-        eye = jnp.where(lane == subn + 8 * m, 1.0, 0.0).astype(jnp.float32)
+        eye = jnp.where(lane == sub[:, :n] + 8 * m, 1.0, 0.0).astype(jnp.float32)
         rows.append(jnp.concatenate([inner[8 * m:8 * m + 8, :], eye], axis=1))
-    full = (8, width)
+
+    def over_lanes(m, j):
+        return jnp.broadcast_to(rows[m][:, j:j + 1], full)
+
+    def over_rows(value, q):
+        return jnp.broadcast_to(value[q:q + 1, :], full)
+
     out = []
+    ahead = {m: [over_lanes(m, p) for p in range(8)] for m in range(2)}
     for k in range(panels):
-        cols = {m: [jnp.broadcast_to(rows[m][:, 8 * k + p:8 * k + p + 1], full) for p in range(8)] for m in range(k, panels)}
-        D = {}
+        later = range(k + 1, panels)
+        cols = dict(ahead)
+        for m in later:
+            if m not in cols:
+                cols[m] = [over_lanes(m, 8 * k + p) for p in range(8)]
+        early = {
+            m: [over_lanes(m, 8 * (k + 1) + j) for j in range(8)]
+            for m in range(k + 1, min(k + 3, panels))
+        }
+        row = [over_rows(rows[k], p) for p in range(8)]
+        diag = {(q, p): over_rows(cols[k][p], q) for p in range(8) for q in range(p, 8)}
+        inv = []
         for p in range(8):
-            for q in range(p, 8):
-                D[q, p] = jnp.broadcast_to(cols[k][p][q:q + 1, :], full)
-        row = [jnp.broadcast_to(rows[k][p:p + 1, :], full) for p in range(8)]
-        dinv = []
-        for p in range(8):
-            dinv.append(1.0 / D[p, p])
+            inv.append(1.0 / diag[p, p])
             for q in range(p + 1, 8):
-                f = D[q, p] * dinv[p]
+                factor = diag[q, p] * inv[p]
                 for r in range(p + 1, q + 1):
-                    D[q, r] = D[q, r] - f * D[r, p]
-                row[q] = row[q] - f * row[p]
-                for m in range(k + 1, panels):
-                    cols[m][q] = cols[m][q] - f * cols[m][p]
-        for m in range(k + 1, panels):
-            acc = rows[m]
-            for p in range(8):
-                acc = acc - (cols[m][p] * dinv[p]) * row[p]
-            rows[m] = acc
-        res = row[0] * lax.rsqrt(D[0, 0])
+                    diag[q, r] = diag[q, r] - factor * diag[r, p]
+                row[q] = row[q] - factor * row[p]
+                for m in later:
+                    cols[m][q] = cols[m][q] - factor * cols[m][p]
+        scaled = {m: [cols[m][p] * inv[p] for p in range(8)] for m in later}
+        ahead = {}
+        if k + 1 < panels:
+            spread = [[over_rows(cols[k + 1][p], j) for p in range(8)] for j in range(8)]
+            for m in early:
+                ahead[m] = []
+                for j in range(8):
+                    value = early[m][j]
+                    for p in range(8):
+                        value = value - scaled[m][p] * spread[j][p]
+                    ahead[m].append(value)
+        for m in later:
+            terms = [scaled[m][p] * row[p] for p in range(8)]
+            while len(terms) > 1:
+                terms = [terms[i] + terms[i + 1] for i in range(0, len(terms), 2)]
+            rows[m] = rows[m] - terms[0]
+        done = row[0] * lax.rsqrt(diag[0, 0])
         for p in range(1, 8):
-            res = jnp.where(sub == p, row[p] * lax.rsqrt(D[p, p]), res)
-        out.append(res[:, n:])
+            done = jnp.where(sub == p, row[p] * lax.rsqrt(diag[p, p]), done)
+        out.append(done[:, n:])
     return jnp.concatenate(out, axis=0)
 
 
 def step_kernel(iters, scale, field_ref, start_ref, out_ref, cols, high, mid, low, half, near, acc,
-                slots, quad, fours, full, gram, work_ref, proj, stage, in_send, in_recv, own_sem,
+                slots, quad, fours, full, gram, work_ref, proj, stage, in_send, in_recv, own_sem, start_sem,
                 core_send, core_recv, plane_send, plane_recv, z_send, z_recv, back_send, back_recv,
                 out_send, out_recv, met):
     x, g, z = lax.axis_index("af"), lax.axis_index("ga"), lax.axis_index("ha")
@@ -93,7 +115,10 @@
         return {"af": lax.rem(x + dx, 4), "ga": lax.rem(g + dg, 8), "ha": lax.rem(z + dz, 16)}
 
     other_core = {"af": x, "ga": g + 1 - 2 * core, "ha": z}
-    plane = [(a, b) for a in range(4) for b in range(4) if (a, b) != (0, 0)]
+    plane = [
+        (2, 2), (1, 2), (3, 2), (2, 1), (2, 3), (1, 1), (1, 3), (3, 1), (3, 3),
+        (2, 0), (0, 2), (1, 0), (3, 0), (0, 1), (0, 3),
+    ]
     sends = []
 
     def send(src, dst, send_sem, recv_sem, device):
@@ -122,6 +147,8 @@
         field_ref.at[:, pl.ds(x * 8, 8), :], cols.at[pl.ds(x * rows, rows)], own_sem
     )
     own.start()
+    first = pltpu.make_async_copy(start_ref, work_ref, start_sem)
+    first.start()
 
     rounds = (
         (at(0, 2, 0), at(0, 6, 0), at(0, 0, 1), at(0, 0, 15)),
@@ -144,6 +171,9 @@
             for ref, part in zip((high, mid, low), parts):
                 ref[pl.ds(p * rows, rows), 128 * s:128 * s + 128] = part
 
+    part = rows // 2
+    swaps, held = [], []
+
     def block(p, q, slot):
         left, right = pl.ds(p * rows, rows), pl.ds(q * rows, rows)
         main = dot16_nt(
@@ -155,6 +185,13 @@
         half[pl.ds(slot * rows, rows), :] = main[:rows, :rows] + (
             (main[:rows, rows:] + main[rows:, :rows]) + small
         )
+        theirs = pl.ds(slot * rows + (1 - core) * part, part)
+        index = len(swaps)
+        swaps.append(send(
+            half.at[theirs], near.at[pl.ds(slot * part, part)],
+            core_send.at[index], core_recv.at[index], other_core,
+        ))
+        held.append(slot)
 
     after, opposite, before = (lax.rem(x + d, 4) for d in (1, 2, 3))
     own.wait()
@@ -179,11 +216,10 @@
     block(pair, pair + 2, 8 + pair)
 
     count = half.shape[0] // 2
-    mine = pl.ds(core * count, count)
-    send(
-        half.at[pl.ds((1 - core) * count, count)], near, core_send.at[0], core_recv.at[0], other_core
-    ).wait_recv()
-    acc[...] = half[mine, :] + near[...]
+    for copy, slot in zip(swaps, held):
+        copy.wait_recv()
+        here = pl.ds(slot * part, part)
+        acc[here, :] = half[pl.ds(slot * rows + core * part, part), :] + near[here, :]
 
     size = count // 16
     me = x * 4 + y
@@ -215,29 +251,37 @@
             copy.wait_recv()
         total = ((ref[0] + ref[1]) + ref[2]) + ref[3]
 
-    here = pl.ds(core * count + me * size, size)
-    full[here, :] = total
+    here = pl.ds(me * size, size)
+    full[core, here, :] = total
     arrivals = [
-        send(full.at[here], full.at[here], back_send.at[i], back_recv.at[i], at(a, 2 * b, 0))
+        send(
+            full.at[core, here], full.at[core, here],
+            back_send.at[i], back_recv.at[i], at(a, 2 * b, 0),
+        )
         for i, (a, b) in enumerate(plane)
     ]
-    for copy in arrivals:
+    swaps = []
+    for i, a in enumerate((0, 1, 3, 2)):
+        for copy, (da, _) in zip(arrivals, plane):
+            if da == (4 - a) % 4:
+                copy.wait_recv()
+        group = pl.ds(lax.rem(x + a, 4) * 4 * size, 4 * size)
+        swaps.append(send(
+            full.at[core, group], full.at[core, group],
+            core_send.at[10 + i], core_recv.at[10 + i], other_core,
+        ))
+    for copy in swaps:
         copy.wait_recv()
-    send(
-        full.at[mine], full.at[mine], core_send.at[1], core_recv.at[1], other_core
-    ).wait_recv()
-    for p in range(4):
-        q = (p + 1) % 4
-        gram[rows * p:rows * p + rows, rows * p:rows * p + rows] = (
-            full[rows * p:rows * p + rows, :] * scale
-        )
-        pairs = [(p, q, 4 + p)] + ([(p, p + 2, 8 + p)] if p < 2 else [])
-        for a, b, slot in pairs:
-            part = full[rows * slot:rows * slot + rows, :] * scale
-            gram[rows * a:rows * a + rows, rows * b:rows * b + rows] = part
-            gram[rows * b:rows * b + rows, rows * a:rows * a + rows] = part.T
-
-    work_ref[...] = dot(start_ref[...], gram[...])
+    pairs = [(p, p, p) for p in range(4)] + [(p, (p + 1) % 4, 4 + p) for p in range(4)]
+    pairs += [(p, p + 2, 8 + p) for p in range(2)]
+    for a, b, slot in pairs:
+        piece = full[:, part * slot:part * slot + part, :].reshape(rows, rows) * scale
+        gram[rows * a:rows * a + rows, rows * b:rows * b + rows] = piece
+        if a != b:
+            gram[rows * b:rows * b + rows, rows * a:rows * a + rows] = piece.T
+
+    first.wait()
+    work_ref[...] = dot(work_ref[...], gram[...])
 
     def step(i, carry):
         work = work_ref[...]
@@ -250,23 +294,25 @@
 
     parts = split(work_ref[...])
     ranks = work_ref.shape[0]
-    main = dot16(jnp.concatenate(parts, axis=0), high[...])
-    middle = dot16(jnp.concatenate(parts[:2], axis=0), mid[...])
-    small = dot16(parts[0], low[...])
-    result = main[:ranks] + (
-        (main[ranks:2 * ranks] + middle[:ranks]) + (middle[ranks:] + (main[2 * ranks:] + small))
-    )
+    share = ranks // 4
     flat_out = proj.reshape(ranks * 8, 128)
-    for s in range(8):
-        flat_out[pl.ds(s, ranks, stride=8), :] = result[:, 128 * s:128 * s + 128]
-    share = ranks // 4
-    arrivals = [
-        send(
-            proj.at[pl.ds(lax.rem(x + d, 4) * share, share)], stage.at[:, pl.ds(x * 8, 8), :],
-            out_send.at[k], out_recv.at[k], at(d, 0, 0),
-        )
-        for k, d in enumerate((2, 1, 3))
-    ]
+    arrivals = []
+    for h in range(2):
+        wide = slice(512 * h, 512 * h + 512)
+        main = dot16(jnp.concatenate(parts, axis=0), high[:, wide])
+        middle = dot16(jnp.concatenate(parts[:2], axis=0), mid[:, wide])
+        small = dot16(parts[0], low[:, wide])
+        result = main[:ranks] + (
+            (main[ranks:2 * ranks] + middle[:ranks]) + (middle[ranks:] + (main[2 * ranks:] + small))
+        )
+        for s in range(4):
+            flat_out[pl.ds(4 * h + s, ranks, stride=8), :] = result[:, 128 * s:128 * s + 128]
+        for k, d in enumerate((2, 1, 3)):
+            arrivals.append(send(
+                proj.at[pl.ds(lax.rem(x + d, 4) * share, share), pl.ds(4 * h, 4), :],
+                stage.at[:, pl.ds(x * 8 + 4 * h, 4), :],
+                out_send.at[h, k], out_recv.at[h, k], at(d, 0, 0),
+            ))
     stage[:, pl.ds(x * 8, 8), :] = proj[pl.ds(x * share, share)]
     for copy in arrivals:
         copy.wait_recv()
@@ -284,7 +330,7 @@
     return pl.pallas_call(
         functools.partial(step_kernel, ITERS, 1.0 / ncols),
         out_shape=jax.ShapeDtypeStruct((ranks // 4, 32, 128), f32),
-        in_specs=[pl.BlockSpec(memory_space=pl.ANY), pl.BlockSpec(memory_space=vmem)],
+        in_specs=[pl.BlockSpec(memory_space=pl.ANY)] * 2,
         out_specs=pl.BlockSpec(memory_space=vmem),
         scratch_shapes=[
             vmem((total, 8, 128), f32),
@@ -297,13 +343,13 @@
             vmem((16, piece, rows), f32),
             vmem((4, piece, rows), f32),
             vmem((4, piece, rows), f32),
-            vmem((10 * rows, rows), f32),
+            vmem((2, 5 * rows, rows), f32),
             vmem((total, total), f32),
             vmem((ranks, total), f32),
             vmem((ranks, 8, 128), f32),
             vmem((ranks // 4, 32, 128), f32),
-            dma((3,)), dma((3,)), dma(()), dma((2,)), dma((2,)), dma((15,)), dma((15,)),
-            dma((6,)), dma((6,)), dma((15,)), dma((15,)), dma((3,)), dma((3,)),
+            dma((3,)), dma((3,)), dma(()), dma(()), dma((14,)), dma((14,)), dma((15,)), dma((15,)),
+            dma((6,)), dma((6,)), dma((15,)), dma((15,)), dma((2, 3)), dma((2, 3)),
             pltpu.SemaphoreType.REGULAR((9,)),
         ],
         compiler_params=pltpu.CompilerParams(

time: 93.4 us -> 88.6 us (0.949)
  Pallas kernels: 91.5 us -> 86.8 us
    pallas_call x1, Pallas kernels: 91.5 us -> 86.8 us  [per_device(): pl.pallas_call(functools.partial(step_kernel, ITERS, 1.0 / ncols), out_sh...]
where the time goes in v3:
time: 88.6 us; the launch traced here: 88.4 us
  Pallas kernels  86.8 us (98%)
  local copies, waits for them, and re-layouts  1.67 us (2%)
    pallas_call x1, Pallas kernels, per_device(): pl.pallas_call(functools.partial(step_kernel, ITERS, 1.0 / ncols), out_sh...  86.8 us

profile of v3, /device:TPU:1, one launch (start us, length us, event | category | flops | bytes accessed | tf_op | source)
XLA Modules:
  0.0 88.4 jit_solution(9136033366134354250)
XLA Ops:
  0.0 86.8 %hosvd_step.1 = f32[16,32,128]{2,1,0:T(8,128)} custom-call(f32[128,32,128]{2,1,0:T(8,128)} %field_ref.1, f32[64,512]{1,0:T(8,128)} %bitcast.1), custom_call_target="tpu_custom_call" | custom-call | tf_op jit(solution)/shard_map/hosvd_step/pallas_call | solution.py:330
  86.8 1.7 %copy.4 = f32[16,32,128]{2,1,0:T(8,128)} copy(f32[16,32,128]{2,1,0:T(8,128)} %hosvd_step.1) | data formatting | bytes 524288

commit v4 on v3

--- a/solution.py
+++ b/solution.py
@@ -11,11 +11,7 @@
 HIGHEST = lax.Precision.HIGHEST
 MESH = pl.DeviceIdType.MESH
 NT = (((1,), (1,)), ((), ()))
-VMEM_LIMIT = 56 * 2**20
-
-
-def dot(a, b):
-    return jnp.dot(a, b, precision=HIGHEST, preferred_element_type=jnp.float32)
+VMEM_LIMIT = 32 * 2**20
 
 
 def dot_nt(a, b):
@@ -38,15 +34,33 @@
     return high, mid, low
 
 
+def times(parts, high, mid, low):
+    n = parts[0].shape[0]
+    first = dot16(jnp.concatenate(parts, axis=0), high)
+    second = dot16(jnp.concatenate(parts[:2], axis=0), mid)
+    third = dot16(parts[0], low)
+    return first[:n] + (
+        (first[n:2 * n] + second[:n]) + (second[n:] + (first[2 * n:] + third))
+    )
+
+
+def wide_times(a, b):
+    ah, am, al = split(a)
+    zero = jnp.zeros(b.shape, jnp.bfloat16)
+    bh, bm, bl = (jnp.concatenate([zero, term], axis=0) for term in split(b))
+    left = jnp.concatenate([ah, ah, ah, am, am, al], axis=1)
+    return dot16(left, jnp.concatenate([bh, bm, bl, bh, bm, bh], axis=0))
+
+
 def chol_inverse(inner):
     n = inner.shape[0]
     panels = n // 8
     full = (8, 2 * n)
     sub = lax.broadcasted_iota(jnp.int32, full, 0)
-    lane = lax.broadcasted_iota(jnp.int32, (8, n), 1)
+    lane = lax.broadcasted_iota(jnp.int32, full, 1)
     rows = []
     for m in range(panels):
-        eye = jnp.where(lane == sub[:, :n] + 8 * m, 1.0, 0.0).astype(jnp.float32)
+        eye = jnp.where(lane[:, :n] == sub[:, :n] + 8 * m, 1.0, 0.0).astype(jnp.float32)
         rows.append(jnp.concatenate([inner[8 * m:8 * m + 8, :], eye], axis=1))
 
     def over_lanes(m, j):
@@ -98,12 +112,12 @@
         done = row[0] * lax.rsqrt(diag[0, 0])
         for p in range(1, 8):
             done = jnp.where(sub == p, row[p] * lax.rsqrt(diag[p, p]), done)
-        out.append(done[:, n:])
+        out.append(jnp.where(lane >= n, done, 0.0))
     return jnp.concatenate(out, axis=0)
 
 
 def step_kernel(iters, scale, field_ref, start_ref, out_ref, cols, high, mid, low, half, near, acc,
-                slots, quad, fours, full, gram, work_ref, proj, stage, in_send, in_recv, own_sem, start_sem,
+                slots, quad, fours, full, gram, gram_mid, gram_low, work_ref, proj, stage, in_send, in_recv, own_sem, start_sem,
                 core_send, core_recv, plane_send, plane_recv, z_send, z_recv, back_send, back_recv,
                 out_send, out_recv, met):
     x, g, z = lax.axis_index("af"), lax.axis_index("ga"), lax.axis_index("ha")
@@ -137,12 +151,25 @@
         pl.semaphore_signal(barrier, inc=1, device_id=device, device_id_type=MESH)
     pl.semaphore_wait(barrier, len(nearest))
 
-    for k, d in enumerate((1, 3, 2)):
+    for k, d in enumerate((1, 3)):
         send(
             field_ref.at[:, pl.ds(lax.rem(x + d, 4) * 8, 8), :], cols.at[pl.ds(x * rows, rows)],
             in_send.at[k], in_recv.at[k], at(d, 0, 0),
         )
-    incoming = {d: sends[k] for k, d in enumerate((3, 1, 2))}
+    from_before, from_after = sends
+
+    def send_opposite():
+        to = lax.rem(x + 2, 4)
+        return [
+            send(
+                field_ref.at[:, pl.ds(to * 8 + 4 * h, 4), :],
+                cols.at[pl.ds(x * rows, rows), pl.ds(4 * h, 4), :],
+                in_send.at[2 + h], in_recv.at[2 + h], at(2, 0, 0),
+            )
+            for h in range(2)
+        ]
+
+    from_opposite = send_opposite()
     own = pltpu.make_async_copy(
         field_ref.at[:, pl.ds(x * 8, 8), :], cols.at[pl.ds(x * rows, rows)], own_sem
     )
@@ -156,7 +183,7 @@
         (at(0, 0, 4), at(0, 0, 12)),
     )
     index = 0
-    for devices in rounds:
+    for turn, devices in enumerate(rounds):
         for i, device in enumerate(devices):
             pl.semaphore_signal(met.at[index + i], inc=1, device_id=device, device_id_type=MESH)
         for i in range(len(devices)):
@@ -165,8 +192,8 @@
 
     flat = cols.reshape(4 * rows * 8, 128)
 
-    def ready(p):
-        for s in range(8):
+    def ready(p, start=0, stop=8):
+        for s in range(start, stop):
             parts = split(flat[pl.ds(p * rows * 8 + s, rows, stride=8), :])
             for ref, part in zip((high, mid, low), parts):
                 ref[pl.ds(p * rows, rows), 128 * s:128 * s + 128] = part
@@ -174,17 +201,20 @@
     part = rows // 2
     swaps, held = [], []
 
-    def block(p, q, slot):
+    def block(p, q, slot, begin=0, end=8):
         left, right = pl.ds(p * rows, rows), pl.ds(q * rows, rows)
+        wide = slice(128 * begin, 128 * end)
         main = dot16_nt(
-            jnp.concatenate([high[left, :], mid[left, :]], axis=0),
-            jnp.concatenate([high[right, :], mid[right, :]], axis=0),
+            jnp.concatenate([high[left, wide], mid[left, wide]], axis=0),
+            jnp.concatenate([high[right, wide], mid[right, wide]], axis=0),
         )
-        small = dot16_nt(low[left, :], high[right, :]) + dot16_nt(high[left, :], low[right, :])
-        small += main[rows:, rows:]
-        half[pl.ds(slot * rows, rows), :] = main[:rows, :rows] + (
-            (main[:rows, rows:] + main[rows:, :rows]) + small
-        )
+        small = dot16_nt(low[left, wide], high[right, wide])
+        small += dot16_nt(high[left, wide], low[right, wide]) + main[rows:, rows:]
+        total = main[:rows, :rows] + ((main[:rows, rows:] + main[rows:, :rows]) + small)
+        whole = pl.ds(slot * rows, rows)
+        half[whole, :] = total if begin == 0 else half[whole, :] + total
+        if end < 8:
+            return
         theirs = pl.ds(slot * rows + (1 - core) * part, part)
         index = len(swaps)
         swaps.append(send(
@@ -197,23 +227,25 @@
     own.wait()
     ready(x)
     block(x, x, x)
-    incoming[1].wait_recv()
+    from_after.wait_recv()
     ready(after)
     block(x, after, 4 + x)
     block(after, after, after)
-    incoming[3].wait_recv()
+    from_before.wait_recv()
     ready(before)
     block(before, x, 4 + before)
     block(before, before, before)
     pair = lax.rem(after, 2)
     block(pair, pair + 2, 8 + pair)
-    incoming[2].wait_recv()
-    ready(opposite)
-    block(after, opposite, 4 + after)
-    block(opposite, before, 4 + opposite)
-    block(opposite, opposite, opposite)
-    pair = lax.rem(x, 2)
-    block(pair, pair + 2, 8 + pair)
+    for h, copy in enumerate(from_opposite):
+        copy.wait_recv()
+        begin, end = 4 * h, 4 * h + 4
+        ready(opposite, begin, end)
+        block(after, opposite, 4 + after, begin, end)
+        block(opposite, before, 4 + opposite, begin, end)
+        block(opposite, opposite, opposite, begin, end)
+        pair = lax.rem(x, 2)
+        block(pair, pair + 2, 8 + pair, begin, end)
 
     count = half.shape[0] // 2
     for copy, slot in zip(swaps, held):
@@ -276,18 +308,18 @@
     pairs += [(p, p + 2, 8 + p) for p in range(2)]
     for a, b, slot in pairs:
         piece = full[:, part * slot:part * slot + part, :].reshape(rows, rows) * scale
-        gram[rows * a:rows * a + rows, rows * b:rows * b + rows] = piece
-        if a != b:
-            gram[rows * b:rows * b + rows, rows * a:rows * a + rows] = piece.T
+        for p, q, value in ((a, b, piece),) if a == b else ((a, b, piece), (b, a, piece.T)):
+            for ref, term in zip((gram, gram_mid, gram_low), split(value)):
+                ref[rows * p:rows * p + rows, rows * q:rows * q + rows] = term
 
     first.wait()
-    work_ref[...] = dot(work_ref[...], gram[...])
+    work_ref[...] = times(split(work_ref[...]), gram[...], gram_mid[...], gram_low[...])
 
     def step(i, carry):
         work = work_ref[...]
         inverse = chol_inverse(dot_nt(work, work))
-        ahead = dot(work, gram[...])
-        work_ref[...] = dot(inverse, jnp.where(i < iters - 1, ahead, work))
+        ahead = times(split(work), gram[...], gram_mid[...], gram_low[...])
+        work_ref[...] = wide_times(inverse, jnp.where(i < iters - 1, ahead, work))
         return carry
 
     lax.fori_loop(0, iters, step, 0)
@@ -299,12 +331,7 @@
     arrivals = []
     for h in range(2):
         wide = slice(512 * h, 512 * h + 512)
-        main = dot16(jnp.concatenate(parts, axis=0), high[:, wide])
-        middle = dot16(jnp.concatenate(parts[:2], axis=0), mid[:, wide])
-        small = dot16(parts[0], low[:, wide])
-        result = main[:ranks] + (
-            (main[ranks:2 * ranks] + middle[:ranks]) + (middle[ranks:] + (main[2 * ranks:] + small))
-        )
+        result = times(parts, high[:, wide], mid[:, wide], low[:, wide])
         for s in range(4):
             flat_out[pl.ds(4 * h + s, ranks, stride=8), :] = result[:, 128 * s:128 * s + 128]
         for k, d in enumerate((2, 1, 3)):
@@ -330,7 +357,7 @@
     return pl.pallas_call(
         functools.partial(step_kernel, ITERS, 1.0 / ncols),
         out_shape=jax.ShapeDtypeStruct((ranks // 4, 32, 128), f32),
-        in_specs=[pl.BlockSpec(memory_space=pl.ANY)] * 2,
+        in_specs=[pl.BlockSpec(memory_space=pltpu.HBM)] * 2,
         out_specs=pl.BlockSpec(memory_space=vmem),
         scratch_shapes=[
             vmem((total, 8, 128), f32),
@@ -344,11 +371,13 @@
             vmem((4, piece, rows), f32),
             vmem((4, piece, rows), f32),
             vmem((2, 5 * rows, rows), f32),
-            vmem((total, total), f32),
+            vmem((total, total), jnp.bfloat16),
+            vmem((total, total), jnp.bfloat16),
+            vmem((total, total), jnp.bfloat16),
             vmem((ranks, total), f32),
             vmem((ranks, 8, 128), f32),
             vmem((ranks // 4, 32, 128), f32),
-            dma((3,)), dma((3,)), dma(()), dma(()), dma((14,)), dma((14,)), dma((15,)), dma((15,)),
+            dma((4,)), dma((4,)), dma(()), dma(()), dma((14,)), dma((14,)), dma((15,)), dma((15,)),
             dma((6,)), dma((6,)), dma((15,)), dma((15,)), dma((2, 3)), dma((2, 3)),
             pltpu.SemaphoreType.REGULAR((9,)),
         ],
@@ -356,7 +385,10 @@
             collective_id=0, has_side_effects=True, vmem_limit_bytes=VMEM_LIMIT
         ),
         name="hosvd_step",
-    )(field, start.T)
+    )(
+        pltpu.with_memory_space_constraint(field, pltpu.HBM),
+        pltpu.with_memory_space_constraint(start.T, pltpu.HBM),
+    )
 
 
 def solution(mesh):

time: 88.6 us -> 84 us (0.948)
  Pallas kernels: 86.8 us -> 83.2 us
  local copies, waits for them, and re-layouts: 1.67 us -> 0.71 us
    pallas_call x1, Pallas kernels: 86.8 us -> 83.2 us  [per_device(): pl.pallas_call(functools.partial(step_kernel, ITERS, 1.0 / ncols), out_sh...]
    unnamed x1, local copies, waits for them, and re-layouts: 1.67 us -> 0.71 us
where the time goes in v4:
time: 84 us; the launch traced here: 83.9 us
  Pallas kernels  83.2 us (99%)
    pallas_call x1, Pallas kernels, per_device(): pl.pallas_call(functools.partial(step_kernel, ITERS, 1.0 / ncols), out_sh...  83.2 us

profile of v4, /device:TPU:1, one launch (start us, length us, event | category | flops | bytes accessed | tf_op | source)
XLA Modules:
  0.0 83.9 jit_solution(10813335087909219653)
XLA Ops:
  0.0 83.2 %hosvd_step.1 = f32[16,32,128]{2,1,0:T(8,128)S(1)} custom-call(f32[128,32,128]{2,1,0:T(8,128)} %field_ref.1, f32[64,512]{1,0:T(8,128)} %bitcast.1), custom_call_target="tpu_custom_call" | custom-call | tf_op jit(solution)/shard_map/hosvd_step/pallas_call | solution.py:357
  83.2 0.7 copy.4

commit v5 on v4

--- a/solution.py
+++ b/solution.py
@@ -117,7 +117,7 @@
 
 
 def step_kernel(iters, scale, field_ref, start_ref, out_ref, cols, high, mid, low, half, near, acc,
-                slots, quad, fours, full, gram, gram_mid, gram_low, work_ref, proj, stage, in_send, in_recv, own_sem, start_sem,
+                slots, quad, fours, full, gram, gram_mid, gram_low, work_ref, proj, in_send, in_recv, own_sem, start_sem,
                 core_send, core_recv, plane_send, plane_recv, z_send, z_recv, back_send, back_recv,
                 out_send, out_recv, met):
     x, g, z = lax.axis_index("af"), lax.axis_index("ga"), lax.axis_index("ha")
@@ -162,11 +162,11 @@
         to = lax.rem(x + 2, 4)
         return [
             send(
-                field_ref.at[:, pl.ds(to * 8 + 4 * h, 4), :],
-                cols.at[pl.ds(x * rows, rows), pl.ds(4 * h, 4), :],
+                field_ref.at[:, pl.ds(to * 8 + 2 * h, 2), :],
+                cols.at[pl.ds(x * rows, rows), pl.ds(2 * h, 2), :],
                 in_send.at[2 + h], in_recv.at[2 + h], at(2, 0, 0),
             )
-            for h in range(2)
+            for h in range(4)
         ]
 
     from_opposite = send_opposite()
@@ -239,7 +239,7 @@
     block(pair, pair + 2, 8 + pair)
     for h, copy in enumerate(from_opposite):
         copy.wait_recv()
-        begin, end = 4 * h, 4 * h + 4
+        begin, end = 2 * h, 2 * h + 2
         ready(opposite, begin, end)
         block(after, opposite, 4 + after, begin, end)
         block(opposite, before, 4 + opposite, begin, end)
@@ -337,13 +337,12 @@
         for k, d in enumerate((2, 1, 3)):
             arrivals.append(send(
                 proj.at[pl.ds(lax.rem(x + d, 4) * share, share), pl.ds(4 * h, 4), :],
-                stage.at[:, pl.ds(x * 8 + 4 * h, 4), :],
+                out_ref.at[:, pl.ds(x * 8 + 4 * h, 4), :],
                 out_send.at[h, k], out_recv.at[h, k], at(d, 0, 0),
             ))
-    stage[:, pl.ds(x * 8, 8), :] = proj[pl.ds(x * share, share)]
+    out_ref[:, pl.ds(x * 8, 8), :] = proj[pl.ds(x * share, share)]
     for copy in arrivals:
         copy.wait_recv()
-    out_ref[...] = stage[...]
     for copy in sends:
         copy.wait_send()
 
@@ -376,8 +375,7 @@
             vmem((total, total), jnp.bfloat16),
             vmem((ranks, total), f32),
             vmem((ranks, 8, 128), f32),
-            vmem((ranks // 4, 32, 128), f32),
-            dma((4,)), dma((4,)), dma(()), dma(()), dma((14,)), dma((14,)), dma((15,)), dma((15,)),
+            dma((6,)), dma((6,)), dma(()), dma(()), dma((14,)), dma((14,)), dma((15,)), dma((15,)),
             dma((6,)), dma((6,)), dma((15,)), dma((15,)), dma((2, 3)), dma((2, 3)),
             pltpu.SemaphoreType.REGULAR((9,)),
         ],

time: 84 us -> 83.7 us (level)
  no operation moved by 1% of the time
where the time goes in v5:
time: 83.7 us; the launch traced here: 83.6 us
  Pallas kernels  82.9 us (99%)
    pallas_call x1, Pallas kernels, per_device(): pl.pallas_call(functools.partial(step_kernel, ITERS, 1.0 / ncols), out_sh...  82.9 us

profile of v5, /device:TPU:1, one launch (start us, length us, event | category | flops | bytes accessed | tf_op | source)
XLA Modules:
  0.0 83.6 jit_solution(6209381435634295117)
XLA Ops:
  0.0 82.9 %hosvd_step.1 = f32[16,32,128]{2,1,0:T(8,128)S(1)} custom-call(f32[128,32,128]{2,1,0:T(8,128)} %field_ref.1, f32[64,512]{1,0:T(8,128)} %bitcast.1), custom_call_target="tpu_custom_call" | custom-call | tf_op jit(solution)/shard_map/hosvd_step/pallas_call | solution.py:356
  82.9 0.7 copy.4

commit v6 on v5

--- a/solution.py
+++ b/solution.py
@@ -293,15 +293,22 @@
         for i, (a, b) in enumerate(plane)
     ]
     swaps = []
-    for i, a in enumerate((0, 1, 3, 2)):
+
+    def forward(group):
+        index = 10 + len(swaps)
+        swaps.append(send(
+            full.at[core, group], full.at[core, group],
+            core_send.at[index], core_recv.at[index], other_core,
+        ))
+
+    for a in (0, 1, 3):
         for copy, (da, _) in zip(arrivals, plane):
             if da == (4 - a) % 4:
                 copy.wait_recv()
-        group = pl.ds(lax.rem(x + a, 4) * 4 * size, 4 * size)
-        swaps.append(send(
-            full.at[core, group], full.at[core, group],
-            core_send.at[10 + i], core_recv.at[10 + i], other_core,
-        ))
+        forward(pl.ds(lax.rem(x + a, 4) * 4 * size, 4 * size))
+    for b in (0, 1, 3, 2):
+        arrivals[plane.index((2, b))].wait_recv()
+        forward(pl.ds((lax.rem(x + 2, 4) * 4 + lax.rem(y + 4 - b, 4)) * size, size))
     for copy in swaps:
         copy.wait_recv()
     pairs = [(p, p, p) for p in range(4)] + [(p, (p + 1) % 4, 4 + p) for p in range(4)]
@@ -375,7 +382,7 @@
             vmem((total, total), jnp.bfloat16),
             vmem((ranks, total), f32),
             vmem((ranks, 8, 128), f32),
-            dma((6,)), dma((6,)), dma(()), dma(()), dma((14,)), dma((14,)), dma((15,)), dma((15,)),
+            dma((6,)), dma((6,)), dma(()), dma(()), dma((17,)), dma((17,)), dma((15,)), dma((15,)),
             dma((6,)), dma((6,)), dma((15,)), dma((15,)), dma((2, 3)), dma((2, 3)),
             pltpu.SemaphoreType.REGULAR((9,)),
         ],

time: 83.7 us -> 83.8 us (level)
  no operation moved by 1% of the time
where the time goes in v6:
time: 83.8 us; the launch traced here: 83.7 us
  Pallas kernels  83 us (99%)
    pallas_call x1, Pallas kernels, per_device(): pl.pallas_call(functools.partial(step_kernel, ITERS, 1.0 / ncols), out_sh...  83 us

profile of v6, /device:TPU:1, one launch (start us, length us, event | category | flops | bytes accessed | tf_op | source)
XLA Modules:
  0.0 83.7 jit_solution(16030143607360115980)
XLA Ops:
  0.0 83.0 %hosvd_step.1 = f32[16,32,128]{2,1,0:T(8,128)S(1)} custom-call(f32[128,32,128]{2,1,0:T(8,128)} %field_ref.1, f32[64,512]{1,0:T(8,128)} %bitcast.1), custom_call_target="tpu_custom_call" | custom-call | tf_op jit(solution)/shard_map/hosvd_step/pallas_call | solution.py:363
  83.0 0.7 copy.4
